TPU v7x, 32 devices: a whole 2x2x4 slice. The times are simulated.
32 devices in a mesh: dp: 4 (over y, x), seq: 8 (over z, core).
Axes of the slice: x: 2, y: 2, z: 4, core: 2. Of those that a mesh axis runs over, the one named last changes fastest.
Arguments:
- tokens: bfloat16 [4, 3072, 2048], P('dp', 'seq'), may hold values from -32 to 32
- w_qkv: bfloat16 [2048, 3072], P(('dp', 'seq')), may hold values from -1 to 1
- w_out: bfloat16 [1024, 2048], P(('dp', 'seq')), may hold values from -0.1875 to 0.1875
Outputs:
- mixed: bfloat16 [4, 3072, 2048], P('dp', 'seq')
All inputs are finite; a program needn't handle non-finite values.
Results may differ from a plain program's by a relative error of at most 0.007.
Values may be sent and summed in bfloat16 or wider, within the bound.
A program may use at most 64 MiB of HBM per device.

v0:
```python
import math

import jax
import jax.numpy as jnp
from jax import lax
from jax.sharding import PartitionSpec as P

HEADS = 8
HEAD_DIM = 128
COLS = 96


def attend(query, keys, values, allowed):
    scores = jnp.einsum(
        "shqd,shkd->shqk", query, keys, preferred_element_type=jnp.float32
    ) / math.sqrt(query.shape[-1])
    scores = jnp.where(allowed, scores, -jnp.inf)
    top = jnp.max(scores, axis=-1, keepdims=True)
    expo = jnp.exp(scores - top)
    weights = (expo / jnp.sum(expo, axis=-1, keepdims=True)).astype(jnp.bfloat16)
    return jnp.einsum(
        "shqk,shkd->shqd", weights, values, preferred_element_type=jnp.float32
    ).astype(jnp.bfloat16)


def add_rows(left, piece):
    return jnp.dot(left, piece, preferred_element_type=jnp.float32)


def column_heads(packed):
    seq_count, grid_rows, local_cols, count, width = packed.shape
    length = grid_rows * local_cols
    flat = packed.reshape(seq_count, length, count, 3, width // 3)
    flat = jnp.transpose(flat, (0, 2, 3, 1, 4))
    places = jnp.arange(length)
    allowed = (places[:, None] % local_cols == places[None, :] % local_cols) & (
        places[:, None] >= places[None, :]
    )
    result = attend(flat[:, :, 0], flat[:, :, 1], flat[:, :, 2], allowed)
    result = jnp.transpose(result, (0, 2, 1, 3)).reshape(
        seq_count, grid_rows, local_cols, count, width // 3
    )
    return lax.all_to_all(result, "seq", split_axis=1, concat_axis=2, tiled=True)


def on_device(tokens, w_qkv, w_out):
    seq_count, tok_count, width = tokens.shape
    flat = tokens.reshape(seq_count * tok_count, width)
    half = HEADS // 2
    qkv = add_rows(flat, lax.all_gather(w_qkv, ("dp", "seq"), axis=0, tiled=True))
    qkv = qkv.astype(jnp.bfloat16).reshape(seq_count, tok_count, HEADS, 3, HEAD_DIM)
    col_packed = qkv[:, :, half:].reshape(seq_count, tok_count // COLS, COLS, half, 3 * HEAD_DIM)
    col_out = column_heads(
        lax.all_to_all(col_packed, "seq", split_axis=2, concat_axis=1, tiled=True)
    )
    col_out = col_out.reshape(seq_count, tok_count, half, HEAD_DIM)
    row_part = jnp.transpose(qkv[:, :, :half], (0, 2, 3, 1, 4))
    places = jnp.arange(tok_count)
    row_mask = (places[:, None] // COLS == places[None, :] // COLS) & (
        places[:, None] >= places[None, :]
    )
    row_out = attend(row_part[:, :, 0], row_part[:, :, 1], row_part[:, :, 2], row_mask)
    row_out = jnp.transpose(row_out, (0, 2, 1, 3))
    heads_out = jnp.concatenate([row_out, col_out], axis=2).reshape(
        seq_count * tok_count, HEADS * HEAD_DIM
    )
    mixed = add_rows(heads_out, lax.all_gather(w_out, ("dp", "seq"), axis=0, tiled=True))
    return mixed.astype(jnp.bfloat16).reshape(seq_count, tok_count, w_out.shape[1])


def solution(mesh):
    in_specs = (P("dp", "seq", None), P(("dp", "seq"), None), P(("dp", "seq"), None))
    out_specs = P("dp", "seq", None)
    return jax.shard_map(
        on_device, mesh=mesh, in_specs=in_specs, out_specs=out_specs, check_vma=False
    )
```

profile of v0, /device:TPU:0, one launch (start us, length us, event | category | flops | bytes accessed | tf_op | source)
XLA Modules:
  0.0 221.5 jit_solution(15541804398739106051)
XLA Ops:
  6.5 0.0 copy-start
  6.5 0.0 all-gather.3.cloned.1.call-start
  6.5 0.7 all-gather.3.cloned.1.call-update
  7.3 0.0 all-gather.5.cloned.1.call-start
  7.3 0.7 all-gather.5.cloned.1.call-update
  8.0 101.2 %all-gather.3.cloned.1.call-done = bf16[2048,3072]{1,0:T(8,128)(2,1)} async-done(((bf16[64,3072]{1,0:T(8,128)(2,1)}), bf16[2048,3072]{1,0:T(8,128)(2,1)}) %all-gather.3.cloned.1.call-update) | async-done | bytes 12582928 | tf_op jit(solution)/shard_map/all_gather | solution.py:50
  109.2 0.0 copy-done
  109.2 10.9 %convolution_convert_fusion = bf16[384,3072]{1,0:T(8,128)(2,1)} fusion(bf16[2048,3072]{1,0:T(8,128)(2,1)} %all-gather.3.cloned.1.call-done, bf16[1,384,2048]{2,1,0:T(8,128)(2,1)S(1)} %copy-done), kind=kOutput, calls=%fused_computation.2 | convolution fusion | flops 4833017856 | bytes 16515072 | tf_op jit(solution)/shard_map/dot_general | solution.py:27
  120.0 4.3 %copy.33 = bf16[384,3072]{0,1:T(8,128)(2,1)} copy(bf16[384,3072]{1,0:T(8,128)(2,1)} %convolution_convert_fusion) | data formatting | bytes 4718592 | tf_op jit(solution)/shard_map/convert_element_type | solution.py:51
  124.3 3.4 %fusion.36 = (bf16[1,384,4,3,128]{1,4,3,2,0:T(8,128)(2,1)}, bf16[1,384,4,3,128]{1,4,3,2,0:T(8,128)(2,1)}) fusion(bf16[1,384,8,3,128]{1,4,3,2,0:T(8,128)(2,1)} %bitcast.102), kind=kLoop, calls=%fused_computation.57 | loop fusion | bytes 4718592 | tf_op jit(solution)/shard_map/slice | solution.py:57
  127.7 3.3 %reshape.182 = bf16[1,4,96,4,384]{2,1,4,3,0:T(4,128)(2,1)S(1)} reshape(bf16[1,384,4,3,128]{1,4,3,2,0:T(8,128)(2,1)} %get-tuple-element.6) | data formatting | bytes 2359296 | tf_op jit(solution)/shard_map/reshape | solution.py:52
  131.0 2.4 %copy.38 = bf16[1,4,96,4,384]{4,1,3,0,2:T(4,128)(2,1)} copy(bf16[1,4,96,4,384]{2,1,4,3,0:T(4,128)(2,1)S(1)} %reshape.182) | data formatting | bytes 2359296 | tf_op jit(solution)/shard_map/reshape | solution.py:52
  133.4 3.6 %all-to-all-start = ((bf16[1,4,96,4,384]{4,1,3,0,2:T(4,128)(2,1)}), bf16[1,4,96,4,384]{4,1,3,0,2:T(4,128)(2,1)S(1)}, u32[]{:S(2)}, u32[]{:S(2)}) async-start(bf16[1,4,96,4,384]{4,1,3,0,2:T(4,128)(2,1)} %copy.38), calls=%async_computation | async-start | bytes 2359296 | tf_op jit(solution)/shard_map/all_to_all | solution.py:54
  137.0 0.1 fusion.14
  137.1 44.5 %all-to-all-done = bf16[1,4,96,4,384]{4,1,3,0,2:T(4,128)(2,1)S(1)} async-done(((bf16[1,4,96,4,384]{4,1,3,0,2:T(4,128)(2,1)}), bf16[1,4,96,4,384]{4,1,3,0,2:T(4,128)(2,1)S(1)}, u32[]{:S(2)}, u32[]{:S(2)}) %all-to-all-start) | async-done | bytes 1179680 | tf_op jit(solution)/shard_map/all_to_all | solution.py:54
  181.6 0.5 copy.39
  182.1 1.5 copy.40
  183.6 3.4 %reshape.174 = bf16[1,384,4,3,128]{4,3,2,1,0:T(4,128)(2,1)S(1)} reshape(bf16[1,8,4,12,4,384]{5,4,3,2,1,0:T(4,128)(2,1)} %copy.40) | data formatting | bytes 2359296 | tf_op jit(solution)/shard_map/reshape | solution.py:33
  187.0 1.4 copy.55
  188.3 0.0 copy-start.3
  188.3 2.1 fusion.37
  190.5 0.0 copy-done.3
  190.5 1.3 fusion.7
  191.8 0.0 copy-start.1
  191.8 1.0 copy.43
  192.8 3.6 %all-to-all-start.1 = ((bf16[1,32,12,4,128]{4,3,2,0,1:T(4,128)(2,1)}), bf16[1,32,12,4,128]{4,3,2,0,1:T(4,128)(2,1)S(1)}, u32[]{:S(2)}, u32[]{:S(2)}) async-start(bf16[1,32,12,4,128]{4,3,2,0,1:T(4,128)(2,1)} %bitcast.17), calls=%async_computation.1 | async-start | bytes 786432 | tf_op jit(solution)/shard_map/all_to_all | solution.py:43
  196.5 0.1 fusion.15
  196.6 0.0 copy-start.4
  196.6 0.0 copy-done.1
  196.6 1.4 copy.53
  198.1 0.0 copy-done.4
  198.1 0.0 copy-start.2
  198.1 2.1 fusion.38
  200.2 0.0 copy-done.2
  200.2 2.1 fusion.6
  202.4 6.4 %all-to-all-done.1 = bf16[1,32,12,4,128]{4,3,2,0,1:T(4,128)(2,1)S(1)} async-done(((bf16[1,32,12,4,128]{4,3,2,0,1:T(4,128)(2,1)}), bf16[1,32,12,4,128]{4,3,2,0,1:T(4,128)(2,1)S(1)}, u32[]{:S(2)}, u32[]{:S(2)}) %all-to-all-start.1) | async-done | bytes 393248 | tf_op jit(solution)/shard_map/all_to_all | solution.py:43
  208.8 0.1 copy.45
  208.9 0.2 copy.46
  209.1 0.3 copy.47
  209.4 0.1 pad_maximum_fusion
  209.5 0.0 all-gather.5.cloned.1.call-done
  209.5 5.2 %fusion.2 = bf16[1,384,2048]{2,1,0:T(8,128)(2,1)} fusion(bf16[384,1024]{0,1:T(8,128)(2,1)S(1)} %bitcast.110, bf16[1024,2048]{1,0:T(8,128)(2,1)} %all-gather.5.cloned.1.call-done), kind=kOutput, calls=%fused_computation.4 | convolution fusion | flops 1611399168 | bytes 6553600 | tf_op jit(solution)/shard_map/dot_general | solution.py:27
  (2 shorter events, 0.0 us)
Async XLA Ops:
  6.5 102.6 %copy-start = (bf16[1,384,2048]{2,1,0:T(8,128)(2,1)S(1)}, bf16[1,384,2048]{2,1,0:T(8,128)(2,1)}, u32[]{:S(2)}) copy-start(bf16[1,384,2048]{2,1,0:T(8,128)(2,1)} %param.3) | copy-start | bytes 4718596
  6.5 102.6 %all-gather.3.cloned.1.call-start = ((), (), s32[]{:S(2)}) async-start(), calls=%async_computation.2 | async-start | bytes 12976128 | tf_op jit(solution)/shard_map/all_gather | solution.py:50
  7.3 202.2 %all-gather.5.cloned.1.call-start = ((), (), s32[]{:S(2)}) async-start(), calls=%async_computation.3 | async-start | bytes 4325376 | tf_op jit(solution)/shard_map/all_gather | solution.py:67
  133.4 48.2 %all-to-all-start = ((bf16[1,4,96,4,384]{4,1,3,0,2:T(4,128)(2,1)}), bf16[1,4,96,4,384]{4,1,3,0,2:T(4,128)(2,1)S(1)}, u32[]{:S(2)}, u32[]{:S(2)}) async-start(bf16[1,4,96,4,384]{4,1,3,0,2:T(4,128)(2,1)} %copy.38), calls=%async_computation | async-start | bytes 2359296 | tf_op jit(solution)/shard_map/all_to_all | solution.py:54
  188.3 2.1 copy-start.3
  191.8 4.9 %copy-start.1 = (bf16[1,384,4,3,128]{1,4,3,2,0:T(8,128)(2,1)S(1)}, bf16[1,384,4,3,128]{1,4,3,2,0:T(8,128)(2,1)}, u32[]{:S(2)}) copy-start(bf16[1,384,4,3,128]{1,4,3,2,0:T(8,128)(2,1)} %get-tuple-element.5) | copy-start | bytes 3538948
  192.8 15.9 %all-to-all-start.1 = ((bf16[1,32,12,4,128]{4,3,2,0,1:T(4,128)(2,1)}), bf16[1,32,12,4,128]{4,3,2,0,1:T(4,128)(2,1)S(1)}, u32[]{:S(2)}, u32[]{:S(2)}) async-start(bf16[1,32,12,4,128]{4,3,2,0,1:T(4,128)(2,1)} %bitcast.17), calls=%async_computation.1 | async-start | bytes 786432 | tf_op jit(solution)/shard_map/all_to_all | solution.py:43
  196.6 1.5 copy-start.4
  198.1 2.1 copy-start.2
Sparse Core Ops, SparseCore 0:
  10.4 98.7 all-gather.2
  112.2 71.2 all-gather.4
where the time goes:
time: 222 us; the launch traced here: 221 us
  waiting for transfers between devices  153 us (69%)
  matrix products  23.7 us (11%)
  local copies, waits for them, and re-layouts  23.2 us (10%)
  between operations  13.5 us (6%)
  starting transfers between devices  7.24 us (3%)
    all_gather x1, waiting for transfers between devices, on_device(): lax.all_gather(w_qkv, ('dp', 'seq'), axis=0, tiled=True)  101 us
    all_to_all x1, waiting for transfers between devices, on_device(): lax.all_to_all(col_packed, 'seq', split_axis=2, concat_axis=1, tiled=True)  44.5 us
    dot_general x2, matrix products, add_rows(): return jnp.dot(left, piece, preferred_element_type=jnp.float32)  16 us
    all_to_all x1, waiting for transfers between devices, column_heads(): lax.all_to_all(result, 'seq', split_axis=1, concat_axis=2, tiled=True)  6.39 us
    reshape x2, local copies, waits for them, and re-layouts, on_device(): qkv[:, :, half:]  5.68 us
    reshape x2, local copies, waits for them, and re-layouts, column_heads(): flat = packed.reshape(seq_count, length, count, 3, width // 3)  4.77 us
  transfers between devices with their start and end apart: 4, of which 3 were waited for; matrix products, arithmetic and copies ran while one was open for 19% of the time, Pallas kernels for 0%

commit v1 on v0

--- a/solution.py
+++ b/solution.py
@@ -1,8 +1,12 @@
+import functools
 import math
 
 import jax
 import jax.numpy as jnp
+import numpy as np
 from jax import lax
+from jax.experimental import pallas as pl
+from jax.experimental.pallas import tpu as pltpu
 from jax.sharding import PartitionSpec as P
 
 HEADS = 8
@@ -68,9 +72,251 @@
     return mixed.astype(jnp.bfloat16).reshape(seq_count, tok_count, w_out.shape[1])
 
 
+HALF = HEADS // 2
+PACK = 3 * HEAD_DIM
+OUT_CHUNKS = 4
+JOBS = HEADS + OUT_CHUNKS
+MESH = pl.DeviceIdType.MESH
+
+
+def fused(tok_count, width, x_ref, wq_ref, wo_ref, perm_ref, unperm_ref, bias_ref, out_ref,
+          xp, w, wo, qkv, col, col_out, home, heads,
+          z_send, z_recv, f_send, f_recv, s_send, s_recv, c_send, c_recv,
+          a_send, a_recv, b_send, b_recv):
+    dp, seq = lax.axis_index("dp"), lax.axis_index("seq")
+    y, x = dp // 2, dp % 2
+    z, c = seq // 2, seq % 2
+    dp_x, dp_y = 2 * y + (1 - x), 2 * (1 - y) + x
+    share = tok_count // 8
+    chunk = width // OUT_CHUNKS
+
+    barrier = pltpu.get_barrier_semaphore()
+    for step in range(1, 8):
+        pl.semaphore_signal(barrier, inc=1, device_id=(dp, (seq + step) % 8), device_id_type=MESH)
+    for other in (dp_x, dp_y):
+        pl.semaphore_signal(barrier, inc=1, device_id=(other, seq), device_id_type=MESH)
+    pl.semaphore_wait(barrier, 9)
+
+    def send(source, target, s_sem, r_sem, device):
+        return pltpu.make_async_remote_copy(
+            src_ref=source, dst_ref=target, send_sem=s_sem, recv_sem=r_sem,
+            device_id=device, device_id_type=MESH)
+
+    def z_copies(own, full, rows, cols, k):
+        return [send(own.at[:, cols], full.at[y, x, z, c, :, cols],
+                     z_send.at[k, step - 1], z_recv.at[k, step - 1],
+                     (dp, 2 * ((z + step) % 4) + c)) for step in range(1, 4)]
+
+    def first_copies(own, full, rows, cols, k):
+        low, high = pl.ds(0, rows // 2), pl.ds(rows // 2, rows // 2)
+        to_x = full.at[y, x, :, c, low, cols]
+        to_y = full.at[y, x, :, c, high, cols]
+        return [send(to_x, to_x, f_send.at[k, 0], f_recv.at[k, 0], (dp_x, seq)),
+                send(to_y, to_y, f_send.at[k, 1], f_recv.at[k, 1], (dp_y, seq))]
+
+    def second_copies(own, full, rows, cols, k):
+        low, high = pl.ds(0, rows // 2), pl.ds(rows // 2, rows // 2)
+        to_y = full.at[y, :, :, c, low, cols]
+        to_x = full.at[:, x, :, c, high, cols]
+        return [send(to_y, to_y, s_send.at[k, 0], s_recv.at[k, 0], (dp_y, seq)),
+                send(to_x, to_x, s_send.at[k, 1], s_recv.at[k, 1], (dp_x, seq))]
+
+    def core_copies(own, full, rows, cols, k):
+        part = full.at[:, :, :, c, :, cols]
+        return [send(part, part, c_send.at[k], c_recv.at[k], (dp, 2 * z + (1 - c)))]
+
+    def away_copies(k):
+        copies = []
+        for step in range(1, 8):
+            peer = (seq + step) % 8
+            copies.append(send(
+                qkv.at[k, pl.ds(pl.multiple_of(peer * share, 16), share)],
+                col.at[k, pl.ds(pl.multiple_of(seq * share, 16), share)],
+                a_send.at[k, step - 1], a_recv.at[k, step - 1], (dp, peer)))
+        return copies
+
+    def back_copies(k):
+        copies = []
+        for step in range(1, 8):
+            peer = (seq + step) % 8
+            copies.append(send(
+                col_out.at[k, pl.ds(pl.multiple_of(peer * share, 16), share)],
+                home.at[k, pl.ds(pl.multiple_of(seq * share, 16), share)],
+                b_send.at[k, step - 1], b_recv.at[k, step - 1], (dp, peer)))
+        return copies
+
+    def job(make, k, act):
+        @pl.when((k >= 0) & (k < HEADS))
+        def _():
+            cols = pl.ds(pl.multiple_of(((k + HALF) % HEADS) * PACK, 128), PACK)
+            for copy in make(wq_ref, w, wq_ref.shape[0], cols, k):
+                act(copy)
+
+        @pl.when((k >= HEADS) & (k < JOBS))
+        def _():
+            cols = pl.ds(pl.multiple_of((k - HEADS) * chunk, 128), chunk)
+            for copy in make(wo_ref, wo, wo_ref.shape[0], cols, k):
+                act(copy)
+
+    def start(copy):
+        copy.start()
+
+    def arrived(copy):
+        copy.wait_recv()
+
+    def sent(copy):
+        copy.wait_send()
+
+    def attention(packed, bias):
+        query, keys, values = (packed[:, p * HEAD_DIM:(p + 1) * HEAD_DIM] for p in range(3))
+        scores = lax.dot_general(query, keys, (((1,), (1,)), ((), ())),
+                                 preferred_element_type=jnp.float32)
+        scores = scores * (1.0 / math.sqrt(HEAD_DIM)) + bias.astype(jnp.float32)
+        expo = jnp.exp(scores - jnp.max(scores, axis=-1, keepdims=True))
+        weights = expo * (1.0 / jnp.sum(expo, axis=-1, keepdims=True))
+        return jnp.dot(weights.astype(jnp.bfloat16), values,
+                       preferred_element_type=jnp.float32).astype(jnp.bfloat16)
+
+    def reorder(order, block):
+        return jnp.dot(order, block, preferred_element_type=jnp.float32).astype(jnp.bfloat16)
+
+    job(z_copies, jnp.int32(0), start)
+    w[y, x, z, c] = wq_ref[...]
+    wo[y, x, z, c] = wo_ref[...]
+
+    def permute(i, _):
+        cols = pl.ds(pl.multiple_of(i * 512, 128), 512)
+        xp[:, cols] = reorder(perm_ref[...], x_ref[:, cols])
+        return 0
+
+    lax.fori_loop(0, width // 512, permute, 0)
+
+    def body(t, _):
+        job(z_copies, t + 1, start)
+        job(z_copies, jnp.where(t >= 1, t - 1, -1), arrived)
+        job(first_copies, t - 1, start)
+        job(first_copies, t - 2, arrived)
+        job(second_copies, t - 2, start)
+        job(second_copies, t - 3, arrived)
+        job(core_copies, t - 3, start)
+        job(core_copies, t - 4, arrived)
+        k = t - 4
+
+        @pl.when((k >= 0) & (k < HEADS))
+        def _():
+            cols = pl.ds(pl.multiple_of(((k + HALF) % HEADS) * PACK, 128), PACK)
+            weight = w[:, :, :, :, :, cols].reshape(xp.shape[1], PACK)
+            qkv[k] = jnp.dot(xp[...], weight,
+                             preferred_element_type=jnp.float32).astype(jnp.bfloat16)
+
+            @pl.when(k < HALF)
+            def _():
+                for copy in away_copies(k):
+                    copy.start()
+                mine = pl.ds(pl.multiple_of(seq * share, 16), share)
+                col[k, mine] = qkv[k, mine]
+
+            @pl.when(k >= HALF)
+            def _():
+                result = attention(qkv[k], bias_ref[0])
+                heads[:, pl.ds(pl.multiple_of((k - HALF) * HEAD_DIM, 128), HEAD_DIM)] = reorder(
+                    unperm_ref[...], result)
+
+        a = t - 6
+
+        @pl.when((a >= 0) & (a < HALF))
+        def _():
+            for copy in away_copies(a):
+                copy.wait_recv()
+            col_out[a] = attention(col[a], bias_ref[1])
+            for copy in back_copies(a):
+                copy.start()
+            mine = pl.ds(pl.multiple_of(seq * share, 16), share)
+            home[a, mine] = col_out[a, mine]
+
+        b = t - 8
+
+        @pl.when((b >= 0) & (b < HALF))
+        def _():
+            for copy in back_copies(b):
+                copy.wait_recv()
+            heads[:, pl.ds(pl.multiple_of((b + HALF) * HEAD_DIM, 128), HEAD_DIM)] = reorder(
+                unperm_ref[...], home[b])
+
+        @pl.when((k >= HEADS) & (k < JOBS))
+        def _():
+            cols = pl.ds(pl.multiple_of((k - HEADS) * chunk, 128), chunk)
+            weight = wo[:, :, :, :, :, cols].reshape(heads.shape[1], chunk)
+            out_ref[:, cols] = jnp.dot(heads[...], weight,
+                                       preferred_element_type=jnp.float32).astype(jnp.bfloat16)
+        return 0
+
+    lax.fori_loop(0, JOBS + 4, body, 0)
+
+    def drain(k, _):
+        for make in (z_copies, first_copies, second_copies, core_copies):
+            job(make, k, sent)
+        return 0
+
+    lax.fori_loop(0, JOBS, drain, 0)
+
+    def drain_heads(k, _):
+        for copy in away_copies(k) + back_copies(k):
+            copy.wait_send()
+        return 0
+
+    lax.fori_loop(0, HALF, drain_heads, 0)
+
+
+def on_torus(tokens, w_qkv, w_out):
+    _, count, width = tokens.shape
+    rows, share = count // COLS, COLS // 8
+    places = np.arange(count).reshape(rows, 8, share).transpose(1, 0, 2).reshape(count)
+    perm = (places[:, None] == np.arange(count)[None, :])
+    later = np.arange(count)[:, None] >= np.arange(count)[None, :]
+    in_row = (places // COLS)[:, None] == (places // COLS)[None, :]
+    in_col = (np.arange(count) % share)[:, None] == (np.arange(count) % share)[None, :]
+    bias = np.where(np.stack([in_row & later, in_col & later]), 0.0, -np.inf)
+    bf16 = jnp.bfloat16
+    inner = HEADS * HEAD_DIM
+    vmem = pl.BlockSpec(memory_space=pltpu.VMEM)
+    dma = pltpu.SemaphoreType.DMA
+    out = pl.pallas_call(
+        functools.partial(fused, count, width),
+        out_shape=jax.ShapeDtypeStruct((count, width), bf16),
+        in_specs=[vmem] * 6,
+        out_specs=vmem,
+        scratch_shapes=[
+            pltpu.VMEM((count, width), bf16),
+            pltpu.VMEM((2, 2, 4, 2) + w_qkv.shape, bf16),
+            pltpu.VMEM((2, 2, 4, 2) + w_out.shape, bf16),
+            pltpu.VMEM((HEADS, count, PACK), bf16),
+            pltpu.VMEM((HALF, count, PACK), bf16),
+            pltpu.VMEM((HALF, count, HEAD_DIM), bf16),
+            pltpu.VMEM((HALF, count, HEAD_DIM), bf16),
+            pltpu.VMEM((count, inner), bf16),
+            dma((JOBS, 3)), dma((JOBS, 3)),
+            dma((JOBS, 2)), dma((JOBS, 2)),
+            dma((JOBS, 2)), dma((JOBS, 2)),
+            dma((JOBS,)), dma((JOBS,)),
+            dma((HALF, 7)), dma((HALF, 7)),
+            dma((HALF, 7)), dma((HALF, 7)),
+        ],
+        compiler_params=pltpu.CompilerParams(
+            collective_id=0, has_side_effects=True, vmem_limit_bytes=50 * 2**20),
+        cost_estimate=pl.CostEstimate(
+            flops=2 * count * width * (HEADS * PACK + inner),
+            bytes_accessed=4 * count * width, transcendentals=HEADS * count * count),
+    )(tokens.reshape(count, width), w_qkv, w_out, jnp.asarray(perm, bf16),
+      jnp.asarray(perm.T, bf16), jnp.asarray(bias, bf16))
+    return out.reshape(tokens.shape)
+
+
 def solution(mesh):
     in_specs = (P("dp", "seq", None), P(("dp", "seq"), None), P(("dp", "seq"), None))
     out_specs = P("dp", "seq", None)
+    fits = mesh.shape["dp"] == 4 and mesh.shape["seq"] == 8
     return jax.shard_map(
-        on_device, mesh=mesh, in_specs=in_specs, out_specs=out_specs, check_vma=False
-    )
+        on_torus if fits else on_device,
+        mesh=mesh, in_specs=in_specs, out_specs=out_specs, check_vma=False
+    )

time: 222 us -> 112 us (0.50)
  the two profiles are of different devices: /device:TPU:0 before, /device:TPU:25 now
where the time goes in v1:
time: 112 us
  Pallas kernels  106 us (95%)
  local copies, waits for them, and re-layouts  6.03 us (5%)
    pallas_call x1, Pallas kernels, on_torus(): pl.pallas_call(functools.partial(fused, count, width), out_shape=jax.Shap...  106 us
    unnamed x11, local copies, waits for them, and re-layouts  6.03 us

profile of v1, /device:TPU:25, one launch (start us, length us, event | category | flops | bytes accessed | tf_op | source)
XLA Modules:
  0.0 112.0 jit_solution(11014023734923716473)
XLA Ops:
  0.0 0.0 copy-start
  0.0 1.0 copy-done
  1.0 0.0 copy-start.1
  1.0 0.9 copy-done.1
  1.9 0.0 copy-start.2
  1.9 1.1 copy-done.2
  3.0 0.0 copy-start.3
  3.0 1.0 copy-done.3
  3.9 0.0 copy-start.4
  3.9 1.0 copy-done.4
  4.9 105.9 %shard_map.64 = bf16[384,2048]{1,0:T(8,128)(2,1)S(1)} custom-call(bf16[384,2048]{1,0:T(8,128)(2,1)} %bitcast.3, bf16[64,3072]{1,0:T(8,128)(2,1)S(1)} %copy-done, bf16[32,2048]{1,0:T(8,128)(2,1)S(1)} %copy-done.1, bf16[384,384]{1,0:T(8,128)(2,1)S(1)} %copy-done.4, bf16[384,384]{1,0:T(8,128)(2,1)S(1)} %copy-done.3, bf16[2,384,384]{2,1,0:T(8,128)(2,1)S(1)} %copy-done.2), custom_call_target="tpu_custom_call" | custom-call | flops 6442450944 | bytes 3145728 | tf_op jit(solution)/shard_map/pallas_call | solution.py:284
  110.8 1.1 %copy.8 = bf16[1,384,2048]{2,1,0:T(8,128)(2,1)} copy(bf16[1,384,2048]{2,1,0:T(8,128)(2,1)S(1)} %bitcast.2) | data formatting | bytes 3145728
Async XLA Ops:
  0.0 1.0 copy-start
  1.0 0.9 copy-start.1
  1.9 1.1 copy-start.2
  3.0 1.0 copy-start.3
  3.9 1.0 copy-start.4

commit v2 on v1

--- a/solution.py
+++ b/solution.py
@@ -79,8 +79,8 @@
 MESH = pl.DeviceIdType.MESH
 
 
-def fused(tok_count, width, x_ref, wq_ref, wo_ref, perm_ref, unperm_ref, bias_ref, out_ref,
-          xp, w, wo, qkv, col, col_out, home, heads,
+def fused(tok_count, width, x_hbm, wq_ref, wo_ref, perm_hbm, unperm_hbm, bias_hbm, out_ref,
+          x_ref, perm_ref, unperm_ref, bias_ref, l_sem, xp, w, wo, qkv, col, col_out, home, heads,
           z_send, z_recv, f_send, f_recv, s_send, s_recv, c_send, c_recv,
           a_send, a_recv, b_send, b_recv):
     dp, seq = lax.axis_index("dp"), lax.axis_index("seq")
@@ -90,6 +90,12 @@
     share = tok_count // 8
     chunk = width // OUT_CHUNKS
 
+    local = [pltpu.make_async_copy(source, target, l_sem.at[i]) for i, (source, target) in
+             enumerate(((x_hbm, x_ref), (wq_ref, w.at[y, x, z, c]), (wo_ref, wo.at[y, x, z, c]),
+                        (perm_hbm, perm_ref), (unperm_hbm, unperm_ref), (bias_hbm, bias_ref)))]
+    for copy in local:
+        copy.start()
+
     barrier = pltpu.get_barrier_semaphore()
     for step in range(1, 8):
         pl.semaphore_signal(barrier, inc=1, device_id=(dp, (seq + step) % 8), device_id_type=MESH)
@@ -102,10 +108,35 @@
             src_ref=source, dst_ref=target, send_sem=s_sem, recv_sem=r_sem,
             device_id=device, device_id_type=MESH)
 
-    def z_copies(own, full, rows, cols, k):
-        return [send(own.at[:, cols], full.at[y, x, z, c, :, cols],
-                     z_send.at[k, step - 1], z_recv.at[k, step - 1],
-                     (dp, 2 * ((z + step) % 4) + c)) for step in range(1, 4)]
+    def z_copies(hop, own, full, rows, cols, k):
+        below, above = (z + 5 - hop) % 4, (z + hop - 1) % 4
+        up, down = (z + 1) % 4, (z + 3) % 4
+        copies = []
+        for way, (block, target) in enumerate(((below, up), (above, down))):
+            landing = full.at[y, x, block, c, :, cols]
+            slot = 3 * way + hop - 1
+            copies.append(send(own.at[:, cols] if hop == 1 else landing, landing,
+                               z_send.at[k, slot], z_recv.at[k, slot], (dp, 2 * target + c)))
+        return copies
+
+    def z_sends(hop):
+        return [(z < 3) & (z >= hop - 1), (z > 0) & (z <= 4 - hop)]
+
+    def z_receives(hop):
+        return [z >= hop, z <= 3 - hop]
+
+    def z_job(hop, k, act, conditions):
+        def guarded(own, full, rows, cols, k):
+            return list(zip(conditions(hop), z_copies(hop, own, full, rows, cols, k)))
+
+        def run(pair):
+            condition, copy = pair
+
+            @pl.when(condition)
+            def _():
+                act(copy)
+
+        job(guarded, k, run)
 
     def first_copies(own, full, rows, cols, k):
         low, high = pl.ds(0, rows // 2), pl.ds(rows // 2, rows // 2)
@@ -180,20 +211,27 @@
     def reorder(order, block):
         return jnp.dot(order, block, preferred_element_type=jnp.float32).astype(jnp.bfloat16)
 
-    job(z_copies, jnp.int32(0), start)
-    w[y, x, z, c] = wq_ref[...]
-    wo[y, x, z, c] = wo_ref[...]
+    z_job(1, jnp.int32(0), start, z_sends)
+    z_job(1, jnp.int32(1), start, z_sends)
+    for copy in local:
+        copy.wait()
 
     def permute(i, _):
         cols = pl.ds(pl.multiple_of(i * 512, 128), 512)
         xp[:, cols] = reorder(perm_ref[...], x_ref[:, cols])
         return 0
 
+    z_job(1, jnp.int32(0), arrived, z_receives)
+    z_job(2, jnp.int32(0), start, z_sends)
     lax.fori_loop(0, width // 512, permute, 0)
 
     def body(t, _):
-        job(z_copies, t + 1, start)
-        job(z_copies, jnp.where(t >= 1, t - 1, -1), arrived)
+        z_job(1, t + 2, start, z_sends)
+        z_job(1, t + 1, arrived, z_receives)
+        z_job(2, t + 1, start, z_sends)
+        z_job(2, t, arrived, z_receives)
+        z_job(3, t, start, z_sends)
+        z_job(3, t - 1, arrived, z_receives)
         job(first_copies, t - 1, start)
         job(first_copies, t - 2, arrived)
         job(second_copies, t - 2, start)
@@ -254,7 +292,9 @@
     lax.fori_loop(0, JOBS + 4, body, 0)
 
     def drain(k, _):
-        for make in (z_copies, first_copies, second_copies, core_copies):
+        for hop in (1, 2, 3):
+            z_job(hop, k, sent, z_sends)
+        for make in (first_copies, second_copies, core_copies):
             job(make, k, sent)
         return 0
 
@@ -284,9 +324,14 @@
     out = pl.pallas_call(
         functools.partial(fused, count, width),
         out_shape=jax.ShapeDtypeStruct((count, width), bf16),
-        in_specs=[vmem] * 6,
+        in_specs=[pl.BlockSpec(memory_space=pltpu.HBM)] * 6,
         out_specs=vmem,
         scratch_shapes=[
+            pltpu.VMEM((count, width), bf16),
+            pltpu.VMEM((count, count), bf16),
+            pltpu.VMEM((count, count), bf16),
+            pltpu.VMEM((2, count, count), bf16),
+            dma((6,)),
             pltpu.VMEM((count, width), bf16),
             pltpu.VMEM((2, 2, 4, 2) + w_qkv.shape, bf16),
             pltpu.VMEM((2, 2, 4, 2) + w_out.shape, bf16),
@@ -295,7 +340,7 @@
             pltpu.VMEM((HALF, count, HEAD_DIM), bf16),
             pltpu.VMEM((HALF, count, HEAD_DIM), bf16),
             pltpu.VMEM((count, inner), bf16),
-            dma((JOBS, 3)), dma((JOBS, 3)),
+            dma((JOBS, 6)), dma((JOBS, 6)),
             dma((JOBS, 2)), dma((JOBS, 2)),
             dma((JOBS, 2)), dma((JOBS, 2)),
             dma((JOBS,)), dma((JOBS,)),
@@ -303,7 +348,7 @@
             dma((HALF, 7)), dma((HALF, 7)),
         ],
         compiler_params=pltpu.CompilerParams(
-            collective_id=0, has_side_effects=True, vmem_limit_bytes=50 * 2**20),
+            collective_id=0, has_side_effects=True, vmem_limit_bytes=62 * 2**20),
         cost_estimate=pl.CostEstimate(
             flops=2 * count * width * (HEADS * PACK + inner),
             bytes_accessed=4 * count * width, transcendentals=HEADS * count * count),

time: 112 us -> 103 us (0.920)
  the two profiles are of different devices: /device:TPU:25 before, /device:TPU:0 now
where the time goes in v2:
time: 103 us; the launch traced here: 101 us
  Pallas kernels  98.5 us (96%)
  local copies, waits for them, and re-layouts  2.73 us (3%)
    pallas_call x1, Pallas kernels, on_torus(): pl.pallas_call(functools.partial(fused, count, width), out_shape=jax.Shap...  98.5 us
    unnamed x1, local copies, waits for them, and re-layouts  2.73 us

profile of v2, /device:TPU:0, one launch (start us, length us, event | category | flops | bytes accessed | tf_op | source)
XLA Modules:
  0.0 101.2 jit_solution(8032315573786701867)
XLA Ops:
  0.0 98.5 %shard_map.64 = bf16[384,2048]{1,0:T(8,128)(2,1)} custom-call(bf16[384,2048]{1,0:T(8,128)(2,1)} %bitcast.3, bf16[64,3072]{1,0:T(8,128)(2,1)} %wq_ref.1, bf16[32,2048]{1,0:T(8,128)(2,1)} %wo_ref.1, bf16[384,384]{1,0:T(8,128)(2,1)} %constant.6.clone.perm_hbm, bf16[384,384]{1,0:T(8,128)(2,1)} %constant.7.clone.unperm_hbm, ...), custom_call_target="tpu_custom_call" | custom-call | flops 6442450944 | bytes 3145728 | tf_op jit(solution)/shard_map/pallas_call | solution.py:324
  98.5 2.7 %copy.8 = bf16[1,384,2048]{2,1,0:T(8,128)(2,1)} copy(bf16[1,384,2048]{2,1,0:T(8,128)(2,1)} %bitcast.2) | data formatting | bytes 3145728

commit v3 on v2

--- a/solution.py
+++ b/solution.py
@@ -211,6 +211,13 @@
     def reorder(order, block):
         return jnp.dot(order, block, preferred_element_type=jnp.float32).astype(jnp.bfloat16)
 
+    def z_ahead(t):
+        z_job(1, t + 3, start, z_sends)
+        z_job(1, t + 2, arrived, z_receives)
+        z_job(2, t + 2, start, z_sends)
+        z_job(2, t + 1, arrived, z_receives)
+        z_job(3, t + 1, start, z_sends)
+
     z_job(1, jnp.int32(0), start, z_sends)
     z_job(1, jnp.int32(1), start, z_sends)
     for copy in local:
@@ -223,22 +230,23 @@
 
     z_job(1, jnp.int32(0), arrived, z_receives)
     z_job(2, jnp.int32(0), start, z_sends)
+    z_job(1, jnp.int32(2), start, z_sends)
+    z_job(1, jnp.int32(1), arrived, z_receives)
+    z_job(2, jnp.int32(1), start, z_sends)
+    z_job(2, jnp.int32(0), arrived, z_receives)
+    z_job(3, jnp.int32(0), start, z_sends)
     lax.fori_loop(0, width // 512, permute, 0)
 
     def body(t, _):
-        z_job(1, t + 2, start, z_sends)
-        z_job(1, t + 1, arrived, z_receives)
-        z_job(2, t + 1, start, z_sends)
-        z_job(2, t, arrived, z_receives)
-        z_job(3, t, start, z_sends)
         z_job(3, t - 1, arrived, z_receives)
         job(first_copies, t - 1, start)
         job(first_copies, t - 2, arrived)
         job(second_copies, t - 2, start)
-        job(second_copies, t - 3, arrived)
-        job(core_copies, t - 3, start)
-        job(core_copies, t - 4, arrived)
-        k = t - 4
+        job(second_copies, t - 4, arrived)
+        job(core_copies, t - 4, start)
+        z_ahead(t)
+        job(core_copies, t - 5, arrived)
+        k = t - 5
 
         @pl.when((k >= 0) & (k < HEADS))
         def _():
@@ -260,7 +268,7 @@
                 heads[:, pl.ds(pl.multiple_of((k - HALF) * HEAD_DIM, 128), HEAD_DIM)] = reorder(
                     unperm_ref[...], result)
 
-        a = t - 6
+        a = t - 7
 
         @pl.when((a >= 0) & (a < HALF))
         def _():
@@ -272,7 +280,7 @@
             mine = pl.ds(pl.multiple_of(seq * share, 16), share)
             home[a, mine] = col_out[a, mine]
 
-        b = t - 8
+        b = t - 9
 
         @pl.when((b >= 0) & (b < HALF))
         def _():
@@ -289,7 +297,7 @@
                                        preferred_element_type=jnp.float32).astype(jnp.bfloat16)
         return 0
 
-    lax.fori_loop(0, JOBS + 4, body, 0)
+    lax.fori_loop(0, JOBS + 5, body, 0)
 
     def drain(k, _):
         for hop in (1, 2, 3):

time: 103 us -> 95.9 us (0.931)
  Pallas kernels: 98.5 us -> 92.3 us
    pallas_call x1, Pallas kernels: 98.5 us -> 92.3 us  [on_torus(): pl.pallas_call(functools.partial(fused, count, width), out_shape=jax.Shap...]
where the time goes in v3:
time: 95.9 us; the launch traced here: 95.1 us
  Pallas kernels  92.3 us (96%)
  local copies, waits for them, and re-layouts  2.73 us (3%)
    pallas_call x1, Pallas kernels, on_torus(): pl.pallas_call(functools.partial(fused, count, width), out_shape=jax.Shap...  92.3 us
    unnamed x1, local copies, waits for them, and re-layouts  2.73 us

profile of v3, /device:TPU:0, one launch (start us, length us, event | category | flops | bytes accessed | tf_op | source)
XLA Modules:
  0.0 95.1 jit_solution(18413138307656609123)
XLA Ops:
  0.0 92.3 %shard_map.64 = bf16[384,2048]{1,0:T(8,128)(2,1)} custom-call(bf16[384,2048]{1,0:T(8,128)(2,1)} %bitcast.3, bf16[64,3072]{1,0:T(8,128)(2,1)} %wq_ref.1, bf16[32,2048]{1,0:T(8,128)(2,1)} %wo_ref.1, bf16[384,384]{1,0:T(8,128)(2,1)} %constant.6.clone.perm_hbm, bf16[384,384]{1,0:T(8,128)(2,1)} %constant.7.clone.unperm_hbm, ...), custom_call_target="tpu_custom_call" | custom-call | flops 6442450944 | bytes 3145728 | tf_op jit(solution)/shard_map/pallas_call | solution.py:332
  92.3 2.7 %copy.8 = bf16[1,384,2048]{2,1,0:T(8,128)(2,1)} copy(bf16[1,384,2048]{2,1,0:T(8,128)(2,1)} %bitcast.2) | data formatting | bytes 3145728

commit v4 on v3

--- a/solution.py
+++ b/solution.py
@@ -242,11 +242,11 @@
         job(first_copies, t - 1, start)
         job(first_copies, t - 2, arrived)
         job(second_copies, t - 2, start)
-        job(second_copies, t - 4, arrived)
-        job(core_copies, t - 4, start)
+        job(second_copies, t - 5, arrived)
+        job(core_copies, t - 5, start)
         z_ahead(t)
-        job(core_copies, t - 5, arrived)
-        k = t - 5
+        job(core_copies, t - 6, arrived)
+        k = t - 6
 
         @pl.when((k >= 0) & (k < HEADS))
         def _():
@@ -268,7 +268,7 @@
                 heads[:, pl.ds(pl.multiple_of((k - HALF) * HEAD_DIM, 128), HEAD_DIM)] = reorder(
                     unperm_ref[...], result)
 
-        a = t - 7
+        a = t - 9
 
         @pl.when((a >= 0) & (a < HALF))
         def _():
@@ -280,7 +280,7 @@
             mine = pl.ds(pl.multiple_of(seq * share, 16), share)
             home[a, mine] = col_out[a, mine]
 
-        b = t - 9
+        b = t - 11
 
         @pl.when((b >= 0) & (b < HALF))
         def _():
@@ -297,7 +297,7 @@
                                        preferred_element_type=jnp.float32).astype(jnp.bfloat16)
         return 0
 
-    lax.fori_loop(0, JOBS + 5, body, 0)
+    lax.fori_loop(0, JOBS + 6, body, 0)
 
     def drain(k, _):
         for hop in (1, 2, 3):

time: 95.9 us -> 95.7 us (level)
  no operation moved by 1% of the time
where the time goes in v4:
time: 95.7 us; the launch traced here: 95.6 us
  Pallas kernels  92.9 us (97%)
  local copies, waits for them, and re-layouts  2.73 us (3%)
    pallas_call x1, Pallas kernels, on_torus(): pl.pallas_call(functools.partial(fused, count, width), out_shape=jax.Shap...  92.9 us
    unnamed x1, local copies, waits for them, and re-layouts  2.73 us

profile of v4, /device:TPU:0, one launch (start us, length us, event | category | flops | bytes accessed | tf_op | source)
XLA Modules:
  0.0 95.6 jit_solution(7479613107139671753)
XLA Ops:
  0.0 92.9 %shard_map.64 = bf16[384,2048]{1,0:T(8,128)(2,1)} custom-call(bf16[384,2048]{1,0:T(8,128)(2,1)} %bitcast.3, bf16[64,3072]{1,0:T(8,128)(2,1)} %wq_ref.1, bf16[32,2048]{1,0:T(8,128)(2,1)} %wo_ref.1, bf16[384,384]{1,0:T(8,128)(2,1)} %constant.6.clone.perm_hbm, bf16[384,384]{1,0:T(8,128)(2,1)} %constant.7.clone.unperm_hbm, ...), custom_call_target="tpu_custom_call" | custom-call | flops 6442450944 | bytes 3145728 | tf_op jit(solution)/shard_map/pallas_call | solution.py:332
  92.9 2.7 %copy.8 = bf16[1,384,2048]{2,1,0:T(8,128)(2,1)} copy(bf16[1,384,2048]{2,1,0:T(8,128)(2,1)} %bitcast.2) | data formatting | bytes 3145728

commit v5 on v4

--- a/solution.py
+++ b/solution.py
@@ -74,7 +74,7 @@
 
 HALF = HEADS // 2
 PACK = 3 * HEAD_DIM
-OUT_CHUNKS = 4
+OUT_CHUNKS = 8
 JOBS = HEADS + OUT_CHUNKS
 MESH = pl.DeviceIdType.MESH
 

time: 95.7 us -> 105 us (1.097)
  Pallas kernels: 92.9 us -> 102 us
    pallas_call x1, Pallas kernels: 92.9 us -> 102 us  [on_torus(): pl.pallas_call(functools.partial(fused, count, width), out_shape=jax.Shap...]
where the time goes in v5:
time: 105 us; the launch traced here: 104 us
  Pallas kernels  102 us (97%)
  local copies, waits for them, and re-layouts  2.73 us (3%)
    pallas_call x1, Pallas kernels, on_torus(): pl.pallas_call(functools.partial(fused, count, width), out_shape=jax.Shap...  102 us
    unnamed x1, local copies, waits for them, and re-layouts  2.73 us

profile of v5, /device:TPU:0, one launch (start us, length us, event | category | flops | bytes accessed | tf_op | source)
XLA Modules:
  0.0 104.3 jit_solution(9203761921344378546)
XLA Ops:
  0.0 101.6 %shard_map.64 = bf16[384,2048]{1,0:T(8,128)(2,1)} custom-call(bf16[384,2048]{1,0:T(8,128)(2,1)} %bitcast.3, bf16[64,3072]{1,0:T(8,128)(2,1)} %wq_ref.1, bf16[32,2048]{1,0:T(8,128)(2,1)} %wo_ref.1, bf16[384,384]{1,0:T(8,128)(2,1)} %constant.6.clone.perm_hbm, bf16[384,384]{1,0:T(8,128)(2,1)} %constant.7.clone.unperm_hbm, ...), custom_call_target="tpu_custom_call" | custom-call | flops 6442450944 | bytes 3145728 | tf_op jit(solution)/shard_map/pallas_call | solution.py:332
  101.6 2.7 %copy.8 = bf16[1,384,2048]{2,1,0:T(8,128)(2,1)} copy(bf16[1,384,2048]{2,1,0:T(8,128)(2,1)} %bitcast.2) | data formatting | bytes 3145728
